TPU v7x, 32 devices: a whole 2x2x4 slice. The times are simulated.
32 devices in a mesh: groups: 2 (over x), row: 16 (over z, y, core).
Axes of the slice: x: 2, y: 2, z: 4, core: 2. Of those that a mesh axis runs over, the one named last changes fastest.
Arguments:
- gated_hidden_rows: bfloat16 [2, 384, 28672], P(None, 'groups', 'row'), parts along dimension 1, may hold values from -6 to 6
- down_base_weight: bfloat16 [8192, 28672], P('row'), may hold values from -0.03125 to 0.03125
- adapter_input_factor: bfloat16 [8, 64, 28672], P(None, None, 'row'), may hold values from -0.03125 to 0.03125
- adapter_output_weight: bfloat16 [8, 64, 8192], P(None, None, 'row'), may hold values from -0.75 to 0.75
- request_adapter_index: int32 [2, 384], P(None, 'groups'), parts along dimension 1, may hold values from 0 to 7, as said below
Outputs:
- ffn_out: bfloat16 [2, 384, 8192], P(None, 'groups', 'row'), parts along dimension 1
There are 2 independent parts, one for each index of `groups`. A program takes and returns all parts, laid end to end along the dimension named above; an argument that names none is the same for every part. Nothing has to cross between parts.
Inputs may be any that keep to these rules, and one draw needn't show every extreme that they name: `request_adapter_index`: each entry names one of the 8 adapters; adapter 0 is the resident adapter that is merged into the weights.
All inputs are finite; a program needn't handle non-finite values.
Results may differ from a plain program's by a relative error of at most 0.0038.
Values may be sent and summed in bfloat16 or wider, within the bound.
A program may use at most 128 MiB of HBM per device.

v0:
```python
import jax
import jax.numpy as jnp
from jax import lax
from jax.sharding import PartitionSpec as P


def select_both(project_rows, adapter_labels, request_count, rank_index):
    choose = (
        adapter_labels[:, None] == jnp.arange(request_count, dtype=jnp.int32)[None, :]
    ).astype(jnp.float32)
    total = project_rows.shape[0]
    own = jnp.sum(
        project_rows.reshape(total, request_count, rank_index) * choose[:, :, None], axis=1
    )
    return jnp.concatenate([own, project_rows[:, :rank_index]], axis=1)


def expand_factor(shrunk_rows, adapter_labels, adapter_output_weight):
    request_count = adapter_output_weight.shape[0]
    rank_index = adapter_output_weight.shape[1]
    total = shrunk_rows.shape[0]
    choose = (
        adapter_labels[:, None] == jnp.arange(request_count, dtype=jnp.int32)[None, :]
    ).astype(jnp.float32)
    spread = (choose[:, :, None] * shrunk_rows[:, None, :rank_index].astype(jnp.float32)).reshape(
        total, request_count * rank_index
    )
    operand = jnp.concatenate([spread.astype(jnp.bfloat16), shrunk_rows[:, rank_index:]], axis=1)
    stacked_weights = jnp.concatenate(
        [
            adapter_output_weight.reshape(
                request_count * rank_index, adapter_output_weight.shape[2]
            ),
            -adapter_output_weight[0],
        ],
        axis=0,
    )
    return jnp.dot(operand, stacked_weights, preferred_element_type=jnp.float32)


def local(
    gated_hidden_rows,
    down_base_weight,
    adapter_input_factor,
    adapter_output_weight,
    request_adapter_index,
):
    steps, requests, device_units = gated_hidden_rows.shape
    request_count = adapter_input_factor.shape[0]
    rank_index = adapter_input_factor.shape[1]
    flattened_rows = gated_hidden_rows.reshape(steps * requests, device_units)
    adapter_labels = request_adapter_index.reshape(steps * requests)
    project_rows = jnp.dot(
        flattened_rows,
        adapter_input_factor.reshape(request_count * rank_index, device_units).T,
        preferred_element_type=jnp.float32,
    )
    summand = select_both(project_rows, adapter_labels, request_count, rank_index)
    summed = lax.psum(summand, "row")
    keep = (adapter_labels != 0).astype(jnp.float32)[:, None]
    shrunk_rows = (summed * keep).astype(jnp.bfloat16)
    resident_sum = summed[:, rank_index:]
    contract = (((1,), (1,)), ((), ()))
    highest = lax.Precision.HIGHEST
    base = lax.dot_general(
        lax.all_gather(flattened_rows, "row", axis=1, tiled=True),
        down_base_weight,
        contract,
        preferred_element_type=jnp.float32,
    )
    base = base + jnp.dot(
        resident_sum, adapter_output_weight[0].astype(jnp.float32), precision=highest
    )
    adapter_update = expand_factor(shrunk_rows, adapter_labels, adapter_output_weight)
    return (base + adapter_update).astype(jnp.bfloat16).reshape(steps, requests, base.shape[1])


def solution(mesh):
    placed = (
        P(None, "groups", "row"),
        P("row", None),
        P(None, None, "row"),
        P(None, None, "row"),
        P(None, "groups"),
    )
    return jax.shard_map(
        local, mesh=mesh, in_specs=placed, out_specs=P(None, "groups", "row"), check_vma=False
    )
```

profile of v0, /device:TPU:0, one launch (start us, length us, event | category | flops | bytes accessed | tf_op | source)
XLA Modules:
  0.0 248.8 jit_solution(5993442033640294135)
XLA Ops:
  6.5 0.0 copy-start
  6.5 0.0 all-reduce.2.cloned.1.call-start
  6.5 0.9 eq.12
  7.4 0.6 copy-done
  8.1 2.5 fusion.13
  10.5 0.1 multiply_reduce_fusion
  10.6 0.7 pad_maximum_fusion
  11.3 0.0 all-reduce.2.cloned.1.call-update
  11.3 0.0 all-gather.2.cloned.1.call-start
  11.4 0.7 all-gather.2.cloned.1.call-update
  12.1 0.8 bitcast_negate_fusion
  12.9 91.0 %all-reduce.2.cloned.1.call-done = f32[384,128]{0,1:T(8,128)} async-done(((f32[384,128]{0,1:T(8,128)}), f32[384,128]{0,1:T(8,128)}) %all-reduce.2.cloned.1.call-update) | async-done | bytes 196624 | tf_op jit(solution)/shard_map/psum | solution.py:59
  103.9 0.9 multiply_convert_fusion.1
  104.9 0.1 multiply_convert_fusion
  104.9 0.0 copy-start.1
  105.0 113.3 %all-gather.2.cloned.1.call-done = bf16[384,28672]{1,0:T(8,128)(2,1)} async-done(((bf16[384,1792]{1,0:T(8,128)(2,1)}), bf16[384,28672]{1,0:T(8,128)(2,1)}) %all-gather.2.cloned.1.call-update) | async-done | bytes 22020112 | tf_op jit(solution)/shard_map/all_gather | solution.py:66
  218.2 20.0 %fusion.12 = f32[384,512]{1,0:T(8,128)S(1)} fusion(bf16[384,28672]{1,0:T(8,128)(2,1)} %all-gather.2.cloned.1.call-done, bf16[512,28672]{1,0:T(8,128)(2,1)} %param.6), kind=kOutput, calls=%fused_computation.22 | convolution fusion | flops 11274289152 | bytes 52166656 | tf_op jit(solution)/shard_map/dot_general | solution.py:65
  238.3 0.0 copy-done.1
  238.3 1.4 convolution_add_fusion.1
  239.6 2.3 fusion
  (4 shorter events, 0.0 us)
Async XLA Ops:
  6.5 1.5 copy-start
  6.5 97.4 %all-reduce.2.cloned.1.call-start = ((), (), s32[]{:S(2)}) async-start(), calls=%async_computation.1 | async-start | bytes 393216 | tf_op jit(solution)/shard_map/psum | solution.py:59
  11.3 206.9 %all-gather.2.cloned.1.call-start = ((), (), s32[]{:S(2)}) async-start(), calls=%async_computation | async-start | bytes 23396352 | tf_op jit(solution)/shard_map/all_gather | solution.py:66
  104.9 133.3 %copy-start.1 = (f32[384,128]{0,1:T(8,128)S(1)}, f32[384,128]{0,1:T(8,128)}, u32[]{:S(2)}) copy-start(f32[384,128]{0,1:T(8,128)} %all-reduce.2.cloned.1.call-done) | copy-start | bytes 589828
Sparse Core Ops, SparseCore 0:
  11.4 92.4 all-reduce.1
  105.5 112.7 all-gather.1
where the time goes:
time: 249 us
  waiting for transfers between devices  205 us (82%)
  matrix products  26.1 us (10%)
  between operations  13.5 us (5%)
  other arithmetic  2.62 us (1%)
    all_gather x1, waiting for transfers between devices, local(): lax.all_gather(flattened_rows, 'row', axis=1, tiled=True)  113 us
    psum x1, waiting for transfers between devices, local(): summed = lax.psum(summand, 'row')  91 us
    dot_general x1, matrix products, local(): lax.dot_general(lax.all_gather(flattened_rows, 'row', axis=1, tiled=True)...  20 us
  transfers between devices with their start and end apart: 2, of which 2 were waited for; matrix products, arithmetic and copies ran while one was open for 1% of the time, Pallas kernels for 0%

commit v1 on v0

--- a/solution.py
+++ b/solution.py
@@ -1,7 +1,13 @@
+import functools
+
 import jax
 import jax.numpy as jnp
 from jax import lax
+from jax.experimental import pallas as pl
+from jax.experimental.pallas import tpu as pltpu
 from jax.sharding import PartitionSpec as P
+
+CONTRACT = (((1,), (1,)), ((), ()))
 
 
 def select_both(project_rows, adapter_labels, request_count, rank_index):
@@ -38,7 +44,239 @@
     return jnp.dot(operand, stacked_weights, preferred_element_type=jnp.float32)
 
 
+def gather_kernel(Z, NA, CH, x_ref, w_ref, out_ref, hbuf, wbuf, xsem, wsem, rsem, ssem):
+    n = 4 * Z
+    me = lax.axis_index("row")
+    c = lax.rem(me, 2)
+    y = lax.rem(me // 2, 2)
+    z = me // 4
+    units = x_ref.shape[1]
+    RIGHT, LEFT, ACROSS, TWIN = 0, 1, 2, 3
+
+    def blk(zz, yy, cc):
+        return (zz * 2 + yy) * 2 + cc
+
+    target = (
+        blk(jnp.minimum(z + 1, Z - 1), y, c),
+        blk(jnp.maximum(z - 1, 0), y, c),
+        blk(z, 1 - y, c),
+        blk(z, y, 1 - c),
+    )
+    has_right, has_left = z < Z - 1, z > 0
+
+    def remote(k, j, way):
+        rows = pl.ds(pl.multiple_of(j * CH, CH), CH)
+        return pltpu.make_async_remote_copy(
+            src_ref=hbuf.at[k, rows],
+            dst_ref=hbuf.at[k, rows],
+            send_sem=ssem.at[way, k // 2, j],
+            recv_sem=rsem.at[k, j],
+            device_id={"row": target[way]},
+            device_id_type=pl.DeviceIdType.MESH,
+        )
+
+    def arrived(k, j):
+        remote(k, j, TWIN).wait_recv()
+
+    def weight(k):
+        cols = pl.ds(pl.multiple_of(k * units, 128), units)
+        return pltpu.make_async_copy(w_ref.at[:, cols], wbuf.at[k], wsem.at[k])
+
+    own = pltpu.make_async_copy(x_ref, hbuf.at[me], xsem)
+    own.start()
+
+    barrier = pltpu.get_barrier_semaphore()
+
+    def greet(dev):
+        pl.semaphore_signal(
+            barrier, inc=1, device_id={"row": dev}, device_id_type=pl.DeviceIdType.MESH
+        )
+
+    greet(target[ACROSS])
+    greet(target[TWIN])
+
+    @pl.when(has_right)
+    def _():
+        greet(target[RIGHT])
+
+    @pl.when(has_left)
+    def _():
+        greet(target[LEFT])
+
+    pl.semaphore_wait(barrier, 2 + has_right.astype(jnp.int32) + has_left.astype(jnp.int32))
+    own.wait()
+
+    def go_right(k, j):
+        @pl.when(has_right)
+        def _():
+            remote(k, j, RIGHT).start()
+
+    def go_left(k, j):
+        @pl.when(has_left)
+        def _():
+            remote(k, j, LEFT).start()
+
+    remote(me, NA, ACROSS).start()
+
+    @pl.loop(0, NA)
+    def _(j):
+        go_right(me, j)
+        go_left(me, j)
+        remote(me, j, ACROSS).start()
+        remote(me, j, TWIN).start()
+
+    go_right(me, NA)
+    go_left(me, NA)
+    remote(me, NA, TWIN).start()
+
+    @pl.loop(0, n)
+    def _(k):
+        weight(k).start()
+
+    out_ref[...] = jnp.zeros_like(out_ref)
+
+    def from_left(k, j, across):
+        arrived(k, j)
+        go_right(k, j)
+        if across:
+            remote(k, j, ACROSS).start()
+        remote(k, j, TWIN).start()
+
+    def from_right(k, j, across):
+        arrived(k, j)
+        go_left(k, j)
+        if across:
+            remote(k, j, ACROSS).start()
+        remote(k, j, TWIN).start()
+
+    @pl.loop(1, Z + 2)
+    def _(d):
+        zl, zr = z - d, z + d
+        yl, yr = z - (d - 1), z + (d - 1)
+
+        @pl.when(d == 1)
+        def _():
+            k = blk(z, 1 - y, c)
+            arrived(k, NA)
+            go_right(k, NA)
+            go_left(k, NA)
+            remote(k, NA, TWIN).start()
+
+        @pl.loop(0, 8)
+        def _(j):
+            @pl.when(j < NA)
+            def _():
+                @pl.when(zl >= 0)
+                def _():
+                    from_left(blk(zl, y, c), j, True)
+
+                @pl.when(zr < Z)
+                def _():
+                    from_right(blk(zr, y, c), j, True)
+
+                @pl.when(yl >= 0)
+                def _():
+                    k = blk(yl, 1 - y, c)
+                    arrived(k, j)
+                    remote(k, j, TWIN).start()
+
+                @pl.when((yr < Z) & (d > 1))
+                def _():
+                    k = blk(yr, 1 - y, c)
+                    arrived(k, j)
+                    remote(k, j, TWIN).start()
+
+            @pl.when((j == NA) | (j == NA + 1))
+            def _():
+                yy = jnp.where(j == NA, y, 1 - y)
+
+                @pl.when(zl >= 0)
+                def _():
+                    from_left(blk(zl, yy, c), NA, False)
+
+                @pl.when(zr < Z)
+                def _():
+                    from_right(blk(zr, yy, c), NA, False)
+
+            e = d - 1
+            twin, kind = j // 4, lax.rem(j, 4)
+            crossed, up = kind // 2, lax.rem(kind, 2)
+            dist = e - crossed
+            zz = jnp.where(up == 1, z + dist, z - dist)
+            valid = (dist >= 0) & (zz >= 0) & (zz < Z) & ((up == 0) | (dist > 0))
+
+            @pl.when(valid)
+            def _():
+                k = blk(zz, jnp.where(crossed == 1, 1 - y, y), jnp.where(twin == 1, 1 - c, c))
+
+                @pl.when(twin == 1)
+                def _():
+                    @pl.loop(0, NA + 1)
+                    def _(i):
+                        arrived(k, i)
+
+                weight(k).wait()
+                out_ref[...] += lax.dot_general(
+                    hbuf[k], wbuf[k], CONTRACT, preferred_element_type=jnp.float32
+                )
+
+    @pl.loop(0, Z)
+    def _(zz):
+        @pl.loop(0, 2)
+        def _(yy):
+            k = blk(zz, yy, c)
+
+            @pl.loop(0, NA + 1)
+            def _(j):
+                along = (yy == y) | (j == NA)
+
+                @pl.when(has_right & (zz <= z) & along)
+                def _():
+                    remote(k, j, RIGHT).wait_send()
+
+                @pl.when(has_left & (zz >= z) & along)
+                def _():
+                    remote(k, j, LEFT).wait_send()
+
+                @pl.when((yy == y) & ((j < NA) | (zz == z)))
+                def _():
+                    remote(k, j, ACROSS).wait_send()
+
+                remote(k, j, TWIN).wait_send()
+
+
+def gathered_product(n, rows_in, weight):
+    total, units = rows_in.shape
+    features = weight.shape[0]
+    parts = 6
+    chunk = total // parts
+    Z = n // 4
+    return pl.pallas_call(
+        functools.partial(gather_kernel, Z, parts - 1, chunk),
+        out_shape=jax.ShapeDtypeStruct((total, features), jnp.float32),
+        in_specs=[pl.BlockSpec(memory_space=pl.ANY)] * 2,
+        out_specs=pl.BlockSpec(memory_space=pltpu.VMEM),
+        scratch_shapes=[
+            pltpu.VMEM((n, total, units), jnp.bfloat16),
+            pltpu.VMEM((n, features, units), jnp.bfloat16),
+            pltpu.SemaphoreType.DMA,
+            pltpu.SemaphoreType.DMA((n,)),
+            pltpu.SemaphoreType.DMA((n, parts)),
+            pltpu.SemaphoreType.DMA((4, n // 2, parts)),
+        ],
+        compiler_params=pltpu.CompilerParams(
+            collective_id=0, has_side_effects=True, vmem_limit_bytes=60 * 2**20
+        ),
+        cost_estimate=pl.CostEstimate(
+            flops=2 * total * units * n * features,
+            bytes_accessed=2 * n * units * (features + total),
+            transcendentals=0,
+        ),
+    )(rows_in, weight)
+
+
 def local(
+    n,
     gated_hidden_rows,
     down_base_weight,
     adapter_input_factor,
@@ -48,8 +286,9 @@
     steps, requests, device_units = gated_hidden_rows.shape
     request_count = adapter_input_factor.shape[0]
     rank_index = adapter_input_factor.shape[1]
-    flattened_rows = gated_hidden_rows.reshape(steps * requests, device_units)
-    adapter_labels = request_adapter_index.reshape(steps * requests)
+    total = steps * requests
+    flattened_rows = gated_hidden_rows.reshape(total, device_units)
+    adapter_labels = request_adapter_index.reshape(total)
     project_rows = jnp.dot(
         flattened_rows,
         adapter_input_factor.reshape(request_count * rank_index, device_units).T,
@@ -60,14 +299,17 @@
     keep = (adapter_labels != 0).astype(jnp.float32)[:, None]
     shrunk_rows = (summed * keep).astype(jnp.bfloat16)
     resident_sum = summed[:, rank_index:]
-    contract = (((1,), (1,)), ((), ()))
     highest = lax.Precision.HIGHEST
-    base = lax.dot_general(
-        lax.all_gather(flattened_rows, "row", axis=1, tiled=True),
-        down_base_weight,
-        contract,
-        preferred_element_type=jnp.float32,
-    )
+    fits = 2 * n * device_units * (total + down_base_weight.shape[0]) <= 54 * 2**20
+    if n % 4 == 0 and device_units % 128 == 0 and total % 96 == 0 and fits:
+        base = gathered_product(n, flattened_rows, down_base_weight)
+    else:
+        base = lax.dot_general(
+            lax.all_gather(flattened_rows, "row", axis=1, tiled=True),
+            down_base_weight,
+            CONTRACT,
+            preferred_element_type=jnp.float32,
+        )
     base = base + jnp.dot(
         resident_sum, adapter_output_weight[0].astype(jnp.float32), precision=highest
     )
@@ -84,5 +326,9 @@
         P(None, "groups"),
     )
     return jax.shard_map(
-        local, mesh=mesh, in_specs=placed, out_specs=P(None, "groups", "row"), check_vma=False
-    )
+        functools.partial(local, mesh.shape["row"]),
+        mesh=mesh,
+        in_specs=placed,
+        out_specs=P(None, "groups", "row"),
+        check_vma=False,
+    )

time: 249 us -> 147 us (0.59)
  waiting for transfers between devices: 205 us -> 0.04 us
  Pallas kernels: 0 us -> 125 us
  matrix products: 26.1 us -> 5.12 us
    pallas_call x0 -> x1, Pallas kernels: none -> 125 us  [gathered_product(): pl.pallas_call(functools.partial(gather_kernel, Z, parts - 1, chunk), out...]
    all_gather x1 -> x0, waiting for transfers between devices: 113 us -> none  [local(): lax.all_gather(flattened_rows, 'row', axis=1, tiled=True)]
    psum x1, waiting for transfers between devices: 91 us -> 0.02 us  [local(): summed = lax.psum(summand, 'row')]
    dot_general x1 -> x0, matrix products: 20 us -> none  [local(): lax.dot_general(lax.all_gather(flattened_rows, 'row', axis=1, tiled=True)...]
  transfers between devices with their start and end apart: 2 -> 1, of which waited for: 2 -> 0; matrix products, arithmetic and copies ran while one was open for 1% -> 0% of each run, Pallas kernels for 0% -> 85%
where the time goes in v1:
time: 147 us
  Pallas kernels  125 us (85%)
  between operations  13.5 us (9%)
  matrix products  5.12 us (3%)
  local copies, waits for them, and re-layouts  1.9 us (1%)
  other arithmetic  1.85 us (1%)
    pallas_call x1, Pallas kernels, gathered_product(): pl.pallas_call(functools.partial(gather_kernel, Z, parts - 1, chunk), out...  125 us
  transfers between devices with their start and end apart: 1, of which 0 were waited for; matrix products, arithmetic and copies ran while one was open for 0% of the time, Pallas kernels for 85%

profile of v1, /device:TPU:0, one launch (start us, length us, event | category | flops | bytes accessed | tf_op | source)
XLA Modules:
  0.0 146.9 jit_solution(5701801504788030174)
XLA Ops:
  6.5 0.0 copy-start
  6.5 0.0 all-reduce.2.cloned.1.call-start
  6.5 0.9 eq.12
  7.4 0.6 copy-done
  8.1 2.5 %fusion.12 = f32[384,512]{0,1:T(8,128)S(1)} fusion(bf16[384,1792]{1,0:T(8,128)(2,1)} %bitcast.16, bf16[512,1792]{1,0:T(8,128)(2,1)S(1)} %bitcast.12), kind=kOutput, calls=%fused_computation.22 | convolution fusion | flops 704643072 | bytes 3997696 | tf_op jit(solution)/shard_map/dot_general | solution.py:292
  10.5 0.0 copy-start.2
  10.5 0.1 multiply_reduce_fusion
  10.6 0.7 pad_maximum_fusion
  11.3 0.0 all-reduce.2.cloned.1.call-update
  11.3 0.3 copy-done.2
  11.6 124.5 %shard_map.55 = f32[384,512]{1,0:T(8,128)} custom-call(bf16[384,1792]{1,0:T(8,128)(2,1)} %bitcast.17, bf16[512,28672]{1,0:T(8,128)(2,1)} %w_ref.1), custom_call_target="tpu_custom_call" | custom-call | flops 11274289152 | bytes 51380224 | tf_op jit(solution)/shard_map/pallas_call | solution.py:254
  136.2 0.0 copy-start.1
  136.2 0.0 all-reduce.2.cloned.1.call-done
  136.2 1.0 multiply_convert_fusion.1
  137.3 0.1 multiply_convert_fusion
  137.3 0.1 copy-done.1
  137.4 1.4 convolution_add_fusion.1
  138.8 1.2 fusion
  (5 shorter events, 0.0 us)
Async XLA Ops:
  6.5 1.5 %copy-start = (bf16[8,64,1792]{2,1,0:T(8,128)(2,1)S(1)}, bf16[8,64,1792]{2,1,0:T(8,128)(2,1)}, u32[]{:S(2)}) copy-start(bf16[8,64,1792]{2,1,0:T(8,128)(2,1)} %param.7) | copy-start | bytes 5505028
  6.5 129.7 %all-reduce.2.cloned.1.call-start = ((), (), s32[]{:S(2)}) async-start(), calls=%async_computation | async-start | bytes 393216 | tf_op jit(solution)/shard_map/psum | solution.py:298
  10.5 1.1 copy-start.2
  136.2 1.2 copy-start.1
Sparse Core Ops, SparseCore 0:
  11.4 94.9 all-reduce.1

commit v2 on v1

--- a/solution.py
+++ b/solution.py
@@ -44,7 +44,32 @@
     return jnp.dot(operand, stacked_weights, preferred_element_type=jnp.float32)
 
 
-def gather_kernel(Z, NA, CH, x_ref, w_ref, out_ref, hbuf, wbuf, xsem, wsem, rsem, ssem):
+def served_kernel(
+    Z,
+    NA,
+    CH,
+    x_ref,
+    w_ref,
+    a_ref,
+    b_ref,
+    label_ref,
+    out_ref,
+    hbuf,
+    wbuf,
+    acc,
+    labels,
+    sums,
+    totals,
+    half_in,
+    quarter_in,
+    share_in,
+    xsem,
+    wsem,
+    rsem,
+    ssem,
+    part_recv,
+    part_send,
+):
     n = 4 * Z
     me = lax.axis_index("row")
     c = lax.rem(me, 2)
@@ -95,15 +120,13 @@
     greet(target[ACROSS])
     greet(target[TWIN])
 
-    @pl.when(has_right)
-    def _():
-        greet(target[RIGHT])
-
-    @pl.when(has_left)
-    def _():
-        greet(target[LEFT])
-
-    pl.semaphore_wait(barrier, 2 + has_right.astype(jnp.int32) + has_left.astype(jnp.int32))
+    @pl.loop(0, Z)
+    def _(zz):
+        @pl.when(zz != z)
+        def _():
+            greet(blk(zz, y, c))
+
+    pl.semaphore_wait(barrier, Z + 1)
     own.wait()
 
     def go_right(k, j):
@@ -133,7 +156,138 @@
     def _(k):
         weight(k).start()
 
-    out_ref[...] = jnp.zeros_like(out_ref)
+    acc[...] = jnp.zeros_like(acc)
+
+    total, lanes = sums.shape
+    rank = lanes // 2
+    steps, requests = label_ref.shape
+    same = lax.broadcasted_iota(jnp.int32, (requests, requests), 0) == (
+        lax.broadcasted_iota(jnp.int32, (requests, requests), 1)
+    )
+    for s in range(steps):
+        row = label_ref[s : s + 1, :].astype(jnp.float32)
+        column = jnp.sum(jnp.where(same, row, 0.0), axis=1, keepdims=True)
+        labels[s * requests : (s + 1) * requests, :] = jnp.broadcast_to(column, (requests, lanes))
+
+    width = a_ref.shape[0]
+    adapter_of_lane = (lax.broadcasted_iota(jnp.int32, (1, width), 1) // rank).astype(jnp.float32)
+    low = lax.broadcasted_iota(jnp.int32, (1, lanes), 1) < rank
+    projected = lax.dot_general(
+        hbuf[me], a_ref[...], CONTRACT, preferred_element_type=jnp.float32
+    )
+    chosen = jnp.where(adapter_of_lane == labels[:, 0:1], projected, 0.0)
+    folded = sum(chosen[:, i : i + lanes] for i in range(0, width, lanes))
+    own_both = folded + pltpu.roll(folded, rank, 1)
+    sums[...] = jnp.where(low, own_both, pltpu.roll(projected[:, :lanes], rank, 1))
+
+    half, quarter, share = total // 2, total // 4, total // (4 * Z)
+    half_at = c * half
+    quarter_at = half_at + y * quarter
+    share_at = quarter_at + z * share
+
+    def span(start, size):
+        return pl.ds(pl.multiple_of(start, 8), size)
+
+    def part(src, dst, there, slot_in, slot_out):
+        return pltpu.make_async_remote_copy(
+            src_ref=src,
+            dst_ref=dst,
+            send_sem=part_send.at[slot_out],
+            recv_sem=part_recv.at[slot_in],
+            device_id={"row": there},
+            device_id_type=pl.DeviceIdType.MESH,
+        )
+
+    def halves():
+        src = sums.at[span((1 - c) * half, half)]
+        return part(src, half_in, target[TWIN], 0, 0)
+
+    def quarters():
+        src = sums.at[span(half_at + (1 - y) * quarter, quarter)]
+        return part(src, quarter_in, target[ACROSS], 1, 1)
+
+    def shares(zz, mine):
+        src = sums.at[span(quarter_at + zz * share, share)]
+        return part(src, share_in.at[z], blk(zz, y, c), 4 + jnp.where(mine, z, zz), 4 + zz)
+
+    def spread_z(zz, mine):
+        rows = span(share_at, share)
+        slot = 4 + Z + jnp.where(mine, z, zz)
+        return part(totals.at[rows], totals.at[rows], blk(zz, y, c), slot, 4 + Z + zz)
+
+    def spread_y():
+        rows = span(quarter_at, quarter)
+        return part(totals.at[rows], totals.at[rows], target[ACROSS], 2, 2)
+
+    def spread_c():
+        rows = span(half_at, half)
+        return part(totals.at[rows], totals.at[rows], target[TWIN], 3, 3)
+
+    def other_planes(f):
+        @pl.loop(0, Z)
+        def _(zz):
+            @pl.when(zz != z)
+            def _():
+                f(zz)
+
+    halves().start()
+
+    def phase_quarter():
+        halves().wait_recv()
+        sums[span(half_at, half), :] += half_in[...]
+        quarters().start()
+
+    def phase_share():
+        quarters().wait_recv()
+        sums[span(quarter_at, quarter), :] += quarter_in[...]
+        other_planes(lambda zz: shares(zz, True).start())
+
+    def phase_total():
+        other_planes(lambda zz: shares(zz, False).wait_recv())
+        rows = span(share_at, share)
+        totals[rows, :] = sums[rows, :]
+
+        def add(zz):
+            totals[rows, :] += share_in[zz]
+
+        other_planes(add)
+        other_planes(lambda zz: spread_z(zz, True).start())
+
+    def phase_across():
+        other_planes(lambda zz: spread_z(zz, False).wait_recv())
+        spread_y().start()
+
+    def phase_twin():
+        spread_y().wait_recv()
+        spread_c().start()
+
+    def phase_update():
+        spread_c().wait_recv()
+        summed = totals[...]
+        swapped = pltpu.roll(summed, rank, 1)
+        label = labels[:, 0:1]
+        kept = label != 0.0
+        own = jnp.where(low, summed, swapped)
+        resident = jnp.where(low, swapped, summed)
+        own_wide = jnp.concatenate([own] * (width // lanes), axis=1)
+        operand = jnp.where((adapter_of_lane == label) & kept, own_wide, 0.0).astype(jnp.bfloat16)
+        rounded = resident.astype(jnp.bfloat16).astype(jnp.float32)
+        remaining = jnp.where(kept, resident - rounded, resident)
+        upper = remaining.astype(jnp.bfloat16).astype(jnp.float32)
+        pair = jnp.where(low, upper, remaining - upper).astype(jnp.bfloat16)
+        resident_weight = jnp.concatenate([b_ref[0:rank, :], b_ref[0:rank, :]], axis=0)
+        acc[...] += jnp.dot(
+            operand, b_ref[...], preferred_element_type=jnp.float32
+        ) + jnp.dot(pair, resident_weight, preferred_element_type=jnp.float32)
+
+    phases = (
+        (1, 6, phase_quarter),
+        (2, 2, phase_share),
+        (2, 6, phase_total),
+        (3, 2, phase_across),
+        (3, 6, phase_twin),
+        (4, 3, phase_update),
+    )
 
     def from_left(k, j, across):
         arrived(k, j)
@@ -149,10 +303,10 @@
             remote(k, j, ACROSS).start()
         remote(k, j, TWIN).start()
 
-    @pl.loop(1, Z + 2)
+    @pl.loop(1, Z + 3)
     def _(d):
         zl, zr = z - d, z + d
-        yl, yr = z - (d - 1), z + (d - 1)
+        yl, yr = z - (d - 2), z + (d - 2)
 
         @pl.when(d == 1)
         def _():
@@ -174,13 +328,13 @@
                 def _():
                     from_right(blk(zr, y, c), j, True)
 
-                @pl.when(yl >= 0)
+                @pl.when((yl >= 0) & (d > 1))
                 def _():
                     k = blk(yl, 1 - y, c)
                     arrived(k, j)
                     remote(k, j, TWIN).start()
 
-                @pl.when((yr < Z) & (d > 1))
+                @pl.when((yr < Z) & (d > 2))
                 def _():
                     k = blk(yr, 1 - y, c)
                     arrived(k, j)
@@ -198,10 +352,13 @@
                 def _():
                     from_right(blk(zr, yy, c), NA, False)
 
+            for at_d, at_j, phase in phases:
+                pl.when((d == at_d) & (j == at_j))(phase)
+
             e = d - 1
             twin, kind = j // 4, lax.rem(j, 4)
             crossed, up = kind // 2, lax.rem(kind, 2)
-            dist = e - crossed
+            dist = e - 2 * crossed
             zz = jnp.where(up == 1, z + dist, z - dist)
             valid = (dist >= 0) & (zz >= 0) & (zz < Z) & ((up == 0) | (dist > 0))
 
@@ -216,9 +373,11 @@
                         arrived(k, i)
 
                 weight(k).wait()
-                out_ref[...] += lax.dot_general(
+                acc[...] += lax.dot_general(
                     hbuf[k], wbuf[k], CONTRACT, preferred_element_type=jnp.float32
                 )
+
+    out_ref[...] = acc[...].astype(out_ref.dtype)
 
     @pl.loop(0, Z)
     def _(zz):
@@ -244,35 +403,54 @@
 
                 remote(k, j, TWIN).wait_send()
 
-
-def gathered_product(n, rows_in, weight):
+    halves().wait_send()
+    quarters().wait_send()
+    other_planes(lambda zz: shares(zz, True).wait_send())
+    other_planes(lambda zz: spread_z(zz, True).wait_send())
+    spread_y().wait_send()
+    spread_c().wait_send()
+
+
+def served(n, rows_in, weight, factor_in, factor_out, adapter_index):
     total, units = rows_in.shape
     features = weight.shape[0]
+    width = factor_in.shape[0]
+    lanes = 128
     parts = 6
     chunk = total // parts
     Z = n // 4
+    vmem = pl.BlockSpec(memory_space=pltpu.VMEM)
     return pl.pallas_call(
-        functools.partial(gather_kernel, Z, parts - 1, chunk),
-        out_shape=jax.ShapeDtypeStruct((total, features), jnp.float32),
-        in_specs=[pl.BlockSpec(memory_space=pl.ANY)] * 2,
-        out_specs=pl.BlockSpec(memory_space=pltpu.VMEM),
+        functools.partial(served_kernel, Z, parts - 1, chunk),
+        out_shape=jax.ShapeDtypeStruct((total, features), jnp.bfloat16),
+        in_specs=[pl.BlockSpec(memory_space=pl.ANY)] * 2 + [vmem] * 3,
+        out_specs=vmem,
         scratch_shapes=[
             pltpu.VMEM((n, total, units), jnp.bfloat16),
             pltpu.VMEM((n, features, units), jnp.bfloat16),
+            pltpu.VMEM((total, features), jnp.float32),
+            pltpu.VMEM((total, lanes), jnp.float32),
+            pltpu.VMEM((total, lanes), jnp.float32),
+            pltpu.VMEM((total, lanes), jnp.float32),
+            pltpu.VMEM((total // 2, lanes), jnp.float32),
+            pltpu.VMEM((total // 4, lanes), jnp.float32),
+            pltpu.VMEM((Z, total // n, lanes), jnp.float32),
             pltpu.SemaphoreType.DMA,
             pltpu.SemaphoreType.DMA((n,)),
             pltpu.SemaphoreType.DMA((n, parts)),
             pltpu.SemaphoreType.DMA((4, n // 2, parts)),
+            pltpu.SemaphoreType.DMA((4 + 2 * Z,)),
+            pltpu.SemaphoreType.DMA((4 + 2 * Z,)),
         ],
         compiler_params=pltpu.CompilerParams(
-            collective_id=0, has_side_effects=True, vmem_limit_bytes=60 * 2**20
+            collective_id=0, has_side_effects=True, vmem_limit_bytes=62 * 2**20
         ),
         cost_estimate=pl.CostEstimate(
-            flops=2 * total * units * n * features,
+            flops=2 * total * units * (n * features + width),
             bytes_accessed=2 * n * units * (features + total),
             transcendentals=0,
         ),
-    )(rows_in, weight)
+    )(rows_in, weight, factor_in, factor_out, adapter_index)
 
 
 def local(
@@ -288,6 +466,17 @@
     rank_index = adapter_input_factor.shape[1]
     total = steps * requests
     flattened_rows = gated_hidden_rows.reshape(total, device_units)
+    fits = 2 * n * device_units * (total + down_base_weight.shape[0]) <= 54 * 2**20
+    whole_tiles = device_units % 128 == 0 and total % 96 == 0 and total % (8 * n) == 0
+    if n % 16 == 0 and whole_tiles and rank_index == 64 and request_count % 2 == 0 and fits:
+        return served(
+            n,
+            flattened_rows,
+            down_base_weight,
+            adapter_input_factor.reshape(request_count * rank_index, device_units),
+            adapter_output_weight.reshape(request_count * rank_index, down_base_weight.shape[0]),
+            request_adapter_index,
+        ).reshape(steps, requests, down_base_weight.shape[0])
     adapter_labels = request_adapter_index.reshape(total)
     project_rows = jnp.dot(
         flattened_rows,
@@ -300,16 +489,12 @@
     shrunk_rows = (summed * keep).astype(jnp.bfloat16)
     resident_sum = summed[:, rank_index:]
     highest = lax.Precision.HIGHEST
-    fits = 2 * n * device_units * (total + down_base_weight.shape[0]) <= 54 * 2**20
-    if n % 4 == 0 and device_units % 128 == 0 and total % 96 == 0 and fits:
-        base = gathered_product(n, flattened_rows, down_base_weight)
-    else:
-        base = lax.dot_general(
-            lax.all_gather(flattened_rows, "row", axis=1, tiled=True),
-            down_base_weight,
-            CONTRACT,
-            preferred_element_type=jnp.float32,
-        )
+    base = lax.dot_general(
+        lax.all_gather(flattened_rows, "row", axis=1, tiled=True),
+        down_base_weight,
+        CONTRACT,
+        preferred_element_type=jnp.float32,
+    )
     base = base + jnp.dot(
         resident_sum, adapter_output_weight[0].astype(jnp.float32), precision=highest
     )

time: 147 us -> 136 us (0.925)
  between operations: 13.5 us -> 0.01 us
  Pallas kernels: 125 us -> 134 us
  matrix products: 5.12 us -> 0 us
  other arithmetic: 1.85 us -> 0 us
    pallas_call x1, Pallas kernels: 125 us -> 134 us  [served(): pl.pallas_call(functools.partial(served_kernel, Z, parts - 1, chunk), out...]
    dot_general x3 -> x0, matrix products: 5.12 us -> none  [the longest x1 2.46 us: local(): jnp.dot(flattened_rows, adapter_input_factor.reshape(request_count * rank...]
  transfers between devices with their start and end apart: 1 -> 0, of which waited for: 0 -> 0; matrix products, arithmetic and copies ran while one was open for 0% -> 0% of each run, Pallas kernels for 85% -> 0%
where the time goes in v2:
time: 136 us
  Pallas kernels  134 us (99%)
  local copies, waits for them, and re-layouts  1.77 us (1%)
    pallas_call x1, Pallas kernels, served(): pl.pallas_call(functools.partial(served_kernel, Z, parts - 1, chunk), out...  134 us

profile of v2, /device:TPU:0, one launch (start us, length us, event | category | flops | bytes accessed | tf_op | source)
XLA Modules:
  0.0 136.0 jit_solution(1912571604674207905)
XLA Ops:
  0.0 134.3 %shard_map.55 = bf16[384,512]{1,0:T(8,128)(2,1)} custom-call(bf16[384,1792]{1,0:T(8,128)(2,1)} %bitcast.6, bf16[512,28672]{1,0:T(8,128)(2,1)} %w_ref.1, bf16[512,1792]{1,0:T(8,128)(2,1)} %bitcast.5, bf16[512,512]{1,0:T(8,128)(2,1)} %bitcast.7, s32[2,192]{1,0:T(2,128)} %label_ref.1), custom_call_target="tpu_custom_call" | custom-call | flops 11978932224 | bytes 51380224 | tf_op jit(solution)/shard_map/pallas_call | solution.py:423
  134.3 1.8 %copy.7 = bf16[2,192,512]{2,1,0:T(8,128)(2,1)} copy(bf16[2,192,512]{2,1,0:T(8,128)(2,1)} %bitcast.4) | data formatting | bytes 786432

commit v3 on v2

--- a/solution.py
+++ b/solution.py
@@ -63,7 +63,11 @@
     half_in,
     quarter_in,
     share_in,
+    a_buf,
+    b_buf,
     xsem,
+    asem,
+    bsem,
     wsem,
     rsem,
     ssem,
@@ -109,6 +113,10 @@
 
     own = pltpu.make_async_copy(x_ref, hbuf.at[me], xsem)
     own.start()
+    factor_in = pltpu.make_async_copy(a_ref, a_buf, asem)
+    factor_in.start()
+    factor_out = pltpu.make_async_copy(b_ref, b_buf, bsem)
+    factor_out.start()
 
     barrier = pltpu.get_barrier_semaphore()
 
@@ -139,24 +147,21 @@
         def _():
             remote(k, j, LEFT).start()
 
-    remote(me, NA, ACROSS).start()
-
-    @pl.loop(0, NA)
-    def _(j):
+    def along_z(j):
         go_right(me, j)
         go_left(me, j)
-        remote(me, j, ACROSS).start()
+
+    remote(me, NA, ACROSS).start()
+    along_z(0)
+    along_z(1)
+
+    @pl.loop(0, NA + 1)
+    def _(j):
         remote(me, j, TWIN).start()
-
-    go_right(me, NA)
-    go_left(me, NA)
-    remote(me, NA, TWIN).start()
 
     @pl.loop(0, n)
     def _(k):
         weight(k).start()
-
-    acc[...] = jnp.zeros_like(acc)
 
     total, lanes = sums.shape
     rank = lanes // 2
@@ -172,8 +177,9 @@
     width = a_ref.shape[0]
     adapter_of_lane = (lax.broadcasted_iota(jnp.int32, (1, width), 1) // rank).astype(jnp.float32)
     low = lax.broadcasted_iota(jnp.int32, (1, lanes), 1) < rank
+    factor_in.wait()
     projected = lax.dot_general(
-        hbuf[me], a_ref[...], CONTRACT, preferred_element_type=jnp.float32
+        hbuf[me], a_buf[...], CONTRACT, preferred_element_type=jnp.float32
     )
     chosen = jnp.where(adapter_of_lane == labels[:, 0:1], projected, 0.0)
     folded = sum(chosen[:, i : i + lanes] for i in range(0, width, lanes))
@@ -231,6 +237,7 @@
                 f(zz)
 
     halves().start()
+    acc[...] = jnp.zeros_like(acc)
 
     def phase_quarter():
         halves().wait_recv()
@@ -263,6 +270,7 @@
 
     def phase_update():
         spread_c().wait_recv()
+        factor_out.wait()
         summed = totals[...]
         swapped = pltpu.roll(summed, rank, 1)
         label = labels[:, 0:1]
@@ -275,19 +283,29 @@
         remaining = jnp.where(kept, resident - rounded, resident)
         upper = remaining.astype(jnp.bfloat16).astype(jnp.float32)
         pair = jnp.where(low, upper, remaining - upper).astype(jnp.bfloat16)
-        resident_weight = jnp.concatenate([b_ref[0:rank, :], b_ref[0:rank, :]], axis=0)
+        resident_weight = jnp.concatenate([b_buf[0:rank, :], b_buf[0:rank, :]], axis=0)
         acc[...] += jnp.dot(
-            operand, b_ref[...], preferred_element_type=jnp.float32
+            operand, b_buf[...], preferred_element_type=jnp.float32
         ) + jnp.dot(pair, resident_weight, preferred_element_type=jnp.float32)
 
-    phases = (
-        (1, 6, phase_quarter),
-        (2, 2, phase_share),
-        (2, 6, phase_total),
-        (3, 2, phase_across),
-        (3, 6, phase_twin),
-        (4, 3, phase_update),
-    )
+    phase_quarter()
+    remote(me, 0, ACROSS).start()
+    along_z(2)
+    phase_share()
+    remote(me, 1, ACROSS).start()
+    remote(me, 2, ACROSS).start()
+    along_z(3)
+    phase_total()
+
+    @pl.loop(3, NA)
+    def _(j):
+        remote(me, j, ACROSS).start()
+
+    @pl.loop(4, NA + 1)
+    def _(j):
+        along_z(j)
+
+    phases = ((1, 1, phase_across), (1, 7, phase_twin), (2, 3, phase_update))
 
     def from_left(k, j, across):
         arrived(k, j)
@@ -423,7 +441,7 @@
     return pl.pallas_call(
         functools.partial(served_kernel, Z, parts - 1, chunk),
         out_shape=jax.ShapeDtypeStruct((total, features), jnp.bfloat16),
-        in_specs=[pl.BlockSpec(memory_space=pl.ANY)] * 2 + [vmem] * 3,
+        in_specs=[pl.BlockSpec(memory_space=pl.ANY)] * 4 + [vmem],
         out_specs=vmem,
         scratch_shapes=[
             pltpu.VMEM((n, total, units), jnp.bfloat16),
@@ -435,6 +453,10 @@
             pltpu.VMEM((total // 2, lanes), jnp.float32),
             pltpu.VMEM((total // 4, lanes), jnp.float32),
             pltpu.VMEM((Z, total // n, lanes), jnp.float32),
+            pltpu.VMEM((width, units), jnp.bfloat16),
+            pltpu.VMEM((width, features), jnp.bfloat16),
+            pltpu.SemaphoreType.DMA,
+            pltpu.SemaphoreType.DMA,
             pltpu.SemaphoreType.DMA,
             pltpu.SemaphoreType.DMA((n,)),
             pltpu.SemaphoreType.DMA((n, parts)),

time: 136 us -> 130 us (0.956)
  Pallas kernels: 134 us -> 128 us
    pallas_call x1, Pallas kernels: 134 us -> 128 us  [served(): pl.pallas_call(functools.partial(served_kernel, Z, parts - 1, chunk), out...]
where the time goes in v3:
time: 130 us
  Pallas kernels  128 us (98%)
  local copies, waits for them, and re-layouts  1.77 us (1%)
    pallas_call x1, Pallas kernels, served(): pl.pallas_call(functools.partial(served_kernel, Z, parts - 1, chunk), out...  128 us

profile of v3, /device:TPU:0, one launch (start us, length us, event | category | flops | bytes accessed | tf_op | source)
XLA Modules:
  0.0 130.0 jit_solution(3283305980591135239)
XLA Ops:
  0.0 128.2 %shard_map.55 = bf16[384,512]{1,0:T(8,128)(2,1)} custom-call(bf16[384,1792]{1,0:T(8,128)(2,1)} %bitcast.6, bf16[512,28672]{1,0:T(8,128)(2,1)} %w_ref.1, bf16[512,1792]{1,0:T(8,128)(2,1)} %bitcast.5, bf16[512,512]{1,0:T(8,128)(2,1)} %bitcast.7, s32[2,192]{1,0:T(2,128)} %label_ref.1), custom_call_target="tpu_custom_call" | custom-call | flops 11978932224 | bytes 51380224 | tf_op jit(solution)/shard_map/pallas_call | solution.py:441
  128.3 1.8 %copy.7 = bf16[2,192,512]{2,1,0:T(8,128)(2,1)} copy(bf16[2,192,512]{2,1,0:T(8,128)(2,1)} %bitcast.4) | data formatting | bytes 786432

commit v4 on v3

--- a/solution.py
+++ b/solution.py
@@ -374,7 +374,7 @@
                 pl.when((d == at_d) & (j == at_j))(phase)
 
             e = d - 1
-            twin, kind = j // 4, lax.rem(j, 4)
+            twin, kind = lax.rem(j, 2), 3 - j // 2
             crossed, up = kind // 2, lax.rem(kind, 2)
             dist = e - 2 * crossed
             zz = jnp.where(up == 1, z + dist, z - dist)

time: 130 us -> 129 us (level)
  no operation moved by 1% of the time
where the time goes in v4:
time: 129 us
  Pallas kernels  127 us (98%)
  local copies, waits for them, and re-layouts  1.77 us (1%)
    pallas_call x1, Pallas kernels, served(): pl.pallas_call(functools.partial(served_kernel, Z, parts - 1, chunk), out...  127 us

profile of v4, /device:TPU:0, one launch (start us, length us, event | category | flops | bytes accessed | tf_op | source)
XLA Modules:
  0.0 128.9 jit_solution(2481270124501294565)
XLA Ops:
  0.0 127.1 %shard_map.55 = bf16[384,512]{1,0:T(8,128)(2,1)} custom-call(bf16[384,1792]{1,0:T(8,128)(2,1)} %bitcast.6, bf16[512,28672]{1,0:T(8,128)(2,1)} %w_ref.1, bf16[512,1792]{1,0:T(8,128)(2,1)} %bitcast.5, bf16[512,512]{1,0:T(8,128)(2,1)} %bitcast.7, s32[2,192]{1,0:T(2,128)} %label_ref.1), custom_call_target="tpu_custom_call" | custom-call | flops 11978932224 | bytes 51380224 | tf_op jit(solution)/shard_map/pallas_call | solution.py:441
  127.1 1.8 %copy.7 = bf16[2,192,512]{2,1,0:T(8,128)(2,1)} copy(bf16[2,192,512]{2,1,0:T(8,128)(2,1)} %bitcast.4) | data formatting | bytes 786432
